TPU v7x, 256 devices: a whole 4x4x8 slice. The times are simulated.
256 devices in a mesh: ep: 16 (over z, y_hi), dp: 16 (over y_lo, x, core).
Axes of the slice: x: 4, y: 4 (y_hi: 2, y_lo: 2; y = y_hi * 2 + y_lo), z: 8, core: 2. Of those that a mesh axis runs over, the one named last changes fastest.
Arguments:
- route_experts: int32 [65536, 6], P(('ep', 'dp')), may hold values from 0 to 159, as said below
- route_slots: int32 [65536, 6], P(('ep', 'dp')), may hold values from 0 to 255, as said below
- shared_grad: bfloat16 [65536, 2560], P(('ep', 'dp')), may hold values from -6 to 6
- counts: int32 [16, 256], P('ep', 'dp'), may hold values from 0 to 24, as said below
- slot_inputs: bfloat16 [16, 6144, 2560], P('ep', 'dp'), may hold values from -6 to 6
- gate_pre: bfloat16 [16, 6144, 768], P('ep', 'dp'), may hold values from -6 to 6
- up_pre: bfloat16 [16, 6144, 768], P('ep', 'dp'), may hold values from -6 to 6
- hidden_grad: bfloat16 [16, 6144, 768], P('ep', 'dp'), may hold values from -6 to 6
- slot_prob: float32 [16, 6144], P('ep', 'dp'), may hold values from 0.1 to 1
- gate_master: float32 [16, 2560, 768], P('ep', 'dp'), may hold values from -0.125 to 0.125
- gate_first: bfloat16 [16, 2560, 768], P('ep', 'dp'), may hold values from -18 to 18
- gate_second: bfloat16 [16, 2560, 768], P('ep', 'dp'), may hold values from 0.5 to 20
- up_weight: bfloat16 [16, 2560, 768], P('ep', 'dp'), may hold values from -0.125 to 0.125
Outputs:
- grad_input: bfloat16 [65536, 2560], P(('ep', 'dp'))
- score_grad: bfloat16 [65536, 6], P(('ep', 'dp'))
- new_master: float32 [16, 2560, 768], P('ep', 'dp')
- new_first: bfloat16 [16, 2560, 768], P('ep', 'dp')
- new_second: bfloat16 [16, 2560, 768], P('ep', 'dp')
- new_weights: bfloat16 [16, 2560, 768], P('ep')
Inputs may be any that keep to these rules, and one draw needn't show every extreme that they name: `route_experts`: each token names 6 different experts of the 160; every expert is named by some token; expert x below 16 is held by ep index x. `route_slots`: the number of earlier tokens of the same device that name the same expert; some device has an expert named by all its 256 tokens. `counts`: entry [x, d * 16 + s] is the number of choices of expert x by tokens of the device at ep index s and dp index d with rank below 24, that is min(24, all such choices). For every dp index some expert holds exactly 24 rows from every device. Rows of a block past its count belong to no token.
All inputs are finite; a program needn't handle non-finite values.
Results may differ from a plain program's by a relative error of at most 0.0049.
Values may be sent and summed in bfloat16 or wider, within the bound.
A program may use at most 128 MiB of HBM per device.

v0:
```python
import jax
import jax.numpy as jnp
from jax import lax
from jax.sharding import PartitionSpec as P

first_decay = 0.9
second_decay = 0.95
learn_rate = 0.001
weight_decay = 0.1
adam_eps = 1e-08
first_fix = 1.0 - 0.9**10
second_fix = 1.0 - 0.95**10


def slot_backward(gate_rows, up_rows, grad_rows, prob_rows):
    gate_value = gate_rows.astype(jnp.float32)
    up_value = up_rows.astype(jnp.float32)
    grad_value = grad_rows.astype(jnp.float32)
    gate_sig = jax.nn.sigmoid(gate_value)
    gate_act = gate_value * gate_sig
    slot_score = jnp.sum(grad_value * gate_act * up_value, axis=-1).astype(jnp.bfloat16)
    scaled = prob_rows[:, None] * grad_value
    d_up = (scaled * gate_act).astype(jnp.bfloat16)
    d_gate = (scaled * up_value * gate_sig * (1.0 + gate_value * (1.0 - gate_sig))).astype(
        jnp.bfloat16
    )
    return (d_gate, d_up, slot_score)


def per_device(
    route_experts,
    route_slots,
    shared_grad,
    counts,
    slot_inputs,
    gate_pre,
    up_pre,
    hidden_grad,
    slot_prob,
    gate_master,
    gate_first,
    gate_second,
    up_weight,
):
    senders = lax.axis_size("ep")
    rows_in = slot_inputs[0]
    total_rows = rows_in.shape[0]
    capacity = total_rows // senders
    position = jnp.arange(total_rows, dtype=jnp.int32)
    live_rows = position % capacity < jnp.repeat(
        counts[0], capacity, total_repeat_length=total_rows
    )
    d_gate, d_up, slot_score = slot_backward(gate_pre[0], up_pre[0], hidden_grad[0], slot_prob[0])
    d_gate = jnp.where(live_rows[:, None], d_gate, jnp.zeros_like(d_gate))
    d_up = jnp.where(live_rows[:, None], d_up, jnp.zeros_like(d_up))
    grads_both = jnp.stack([d_gate, d_up])
    weights_both = jnp.stack([gate_master[0].astype(jnp.bfloat16), up_weight[0]])
    slot_grad = jnp.einsum(
        "krh,knh->rn",
        grads_both,
        lax.all_gather(weights_both, "dp", axis=1, tiled=True),
        preferred_element_type=jnp.float32,
    ).astype(jnp.bfloat16)
    weight_grad = lax.psum_scatter(
        lax.dot_general(
            rows_in, d_gate, (((0,), (0,)), ((), ())), preferred_element_type=jnp.float32
        ),
        "dp",
        scatter_dimension=0,
        tiled=True,
    )
    back_rows, back_score = (
        lax.all_to_all(slot_grad, "ep", split_axis=0, concat_axis=0, tiled=True),
        lax.all_to_all(slot_score, "ep", split_axis=0, concat_axis=0, tiled=True),
    )
    moment_one = first_decay * gate_first[0].astype(jnp.float32) + (1.0 - first_decay) * weight_grad
    moment_two = (
        second_decay * gate_second[0].astype(jnp.float32)
        + (1.0 - second_decay) * weight_grad * weight_grad
    )
    direction = moment_one / first_fix / (jnp.sqrt(moment_two / second_fix) + adam_eps)
    master_now = gate_master[0]
    new_master = master_now - learn_rate * (direction + weight_decay * master_now)
    new_weights = lax.all_gather(new_master.astype(jnp.bfloat16), "dp", axis=0, tiled=True)
    served = (route_experts < senders) & (route_slots < capacity)
    target = jnp.where(served, route_experts * capacity + route_slots, -1)
    picker = target[:, :, None] == position[None, None, :]
    combine = jnp.sum(picker.astype(jnp.int32), axis=1).astype(jnp.bfloat16)
    routed = jnp.dot(combine, back_rows, preferred_element_type=jnp.float32)
    grad_input = (shared_grad.astype(jnp.float32) + routed).astype(jnp.bfloat16)
    score_grad = jnp.sum(
        jnp.where(picker, back_score[None, None, :].astype(jnp.float32), jnp.float32(0.0)), axis=2
    ).astype(jnp.bfloat16)
    return (
        grad_input,
        score_grad,
        new_master[None],
        moment_one.astype(jnp.bfloat16)[None],
        moment_two.astype(jnp.bfloat16)[None],
        new_weights[None],
    )


def solution(mesh):
    in_specs = (
        P(("ep", "dp"), None),
        P(("ep", "dp"), None),
        P(("ep", "dp"), None),
        P("ep", "dp"),
        P("ep", "dp", None),
        P("ep", "dp", None),
        P("ep", "dp", None),
        P("ep", "dp", None),
        P("ep", "dp"),
        P("ep", "dp", None),
        P("ep", "dp", None),
        P("ep", "dp", None),
        P("ep", "dp", None),
    )
    out_specs = (
        P(("ep", "dp"), None),
        P(("ep", "dp"), None),
        P("ep", "dp", None),
        P("ep", "dp", None),
        P("ep", "dp", None),
        P("ep", None, None),
    )
    return jax.shard_map(
        per_device, mesh=mesh, in_specs=in_specs, out_specs=out_specs, check_vma=False
    )
```

profile of v0, /device:TPU:1, one launch (start us, length us, event | category | flops | bytes accessed | tf_op | source)
XLA Modules:
  0.0 252.9 jit_solution(13847319462947545470)
XLA Ops:
  7.2 1.9 fusion.39
  9.2 0.7 reduce.2
  9.9 10.9 %fusion.33 = pred[384]{0:T(512)(128)(4,1)S(1)} fusion(pred[384]{0:T(512)(128)(4,1)} %constant.166, pred[384]{0:T(512)(128)(4,1)} %constant.167, pred[384]{0:T(512)(128)(4,1)} %constant.168, pred[384]{0:T(512)(128)(4,1)} %constant.169, pred[384]{0:T(512)(128)(4,1)} %constant.170, pred[384]{0:T(512)(128)(4,1)} %constant.171, pred[384]{0:T(512)(128)(4,1)} %constant.172, ...), kind=kLoop, calls=%fused_computation.56 | loop fusion | flops 8448 | bytes 6208 | tf_op jit(solution)/shard_map/lt | solution.py:50
  20.8 3.0 %broadcast_select_fusion = (bf16[1,384,768]{2,1,0:T(8,128)(2,1)S(1)}, bf16[1,384,768]{2,1,0:T(8,128)(2,1)}) fusion(pred[384]{0:T(512)(128)(4,1)S(1)} %fusion.33, bf16[1,384,768]{2,1,0:T(8,128)(2,1)} %param.20, bf16[1,384,768]{2,1,0:T(8,128)(2,1)} %param.21, bf16[1,384,768]{2,1,0:T(8,128)(2,1)} %param.22, f32[384]{0:T(512)S(1)} %reduce.2), kind=kLoop, calls=%fused_computation.46 | loop fusion | flops 5603328 | bytes 2951040 | tf_op jit(solution)/shard_map/jit(_where)/select_n | solution.py:54
  23.8 0.8 copy-done.1
  24.6 5.3 %convolution_bitcast_fusion = f32[2560,768]{0,1:T(8,128)} fusion(bf16[1,384,2560]{2,1,0:T(8,128)(2,1)S(1)} %copy-done, bf16[1,384,768]{2,1,0:T(8,128)(2,1)S(1)} %get-tuple-element.44), kind=kOutput, calls=%fused_computation | convolution fusion | flops 1509949440 | bytes 10420224 | tf_op jit(solution)/shard_map/dot_general | solution.py:65
  29.9 9.1 %copy.52 = f32[2560,768]{1,0:T(8,128)} copy(f32[2560,768]{0,1:T(8,128)} %convolution_bitcast_fusion) | data formatting | bytes 15728640
  39.1 1.0 copy-done.3
  40.1 0.8 pad_maximum_fusion
  41.3 0.9 copy.46
  42.2 1.9 copy.47
  44.0 71.4 %reduce-scatter.4.cloned.1.call-done = f32[160,768]{1,0:T(8,128)} async-done(((f32[2560,768]{1,0:T(8,128)}), f32[160,768]{1,0:T(8,128)}) %reduce-scatter.4.cloned.1.call-update) | async-done | bytes 491536
  115.4 2.2 copy.53
  117.6 3.0 %fusion.38 = (bf16[160,768]{0,1:T(8,128)(2,1)}, f32[160,768]{0,1:T(8,128)S(1)}, bf16[1,160,768]{1,2,0:T(8,128)(2,1)}, bf16[1,160,768]{1,2,0:T(8,128)(2,1)}) fusion(f32[160,768]{0,1:T(8,128)} %copy.53, bf16[1,160,768]{1,2,0:T(8,128)(2,1)} %copy.47, bf16[1,160,768]{1,2,0:T(8,128)(2,1)} %copy.46, f32[1,160,768]{1,2,0:T(8,128)S(1)} %copy.45), kind=kLoop, calls=%fused_computation.62 | loop fusion | flops 2457600 | bytes 2703360 | tf_op jit(solution)/shard_map/convert_element_type | solution.py:84
  120.6 1.9 copy.48
  122.6 1.9 fusion.9
  124.5 0.7 convert_element_type.135
  125.2 9.1 %all-to-all-start.1 = ((bf16[16,24,1]{1,2,0:T(2,128)(2,1)}), bf16[16,24,1]{1,2,0:T(2,128)(2,1)S(1)}, u32[]{:S(2)}, u32[]{:S(2)}) async-start(bf16[16,24,1]{1,2,0:T(2,128)(2,1)} %convert_element_type.135), calls=%async_computation.1 | async-start | bytes 16384 | tf_op jit(solution)/shard_map/all_to_all | solution.py:74
  134.3 38.8 %all-gather.3.cloned.1.call-done = bf16[2,2560,768]{2,1,0:T(8,128)(2,1)} async-done(((bf16[2,160,768]{2,1,0:T(8,128)(2,1)}), bf16[2,2560,768]{2,1,0:T(8,128)(2,1)}) %all-gather.3.cloned.1.call-update) | async-done | bytes 7864336 | tf_op jit(solution)/shard_map/all_gather | solution.py:61
  173.1 7.9 %fusion = bf16[384,2560]{1,0:T(8,128)(2,1)} fusion(bf16[2,2560,768]{2,1,0:T(8,128)(2,1)} %all-gather.3.cloned.1.call-done, bf16[1,384,768]{2,1,0:T(8,128)(2,1)} %get-tuple-element.45, bf16[1,384,768]{2,1,0:T(8,128)(2,1)S(1)} %copy-done.2), kind=kOutput, calls=%fused_computation.2 | convolution fusion | flops 3021471744 | bytes 11010048 | tf_op jit(solution)/shard_map/krh,knh->rn/dot_general | solution.py:58
  181.6 9.1 %all-to-all-start = ((bf16[16,24,2560]{2,1,0:T(8,128)(2,1)}), bf16[16,24,2560]{2,1,0:T(8,128)(2,1)}, u32[]{:S(2)}, u32[]{:S(2)}) async-start(bf16[16,24,2560]{2,1,0:T(8,128)(2,1)} %bitcast.97), calls=%async_computation | async-start | bytes 3932160 | tf_op jit(solution)/shard_map/all_to_all | solution.py:73
  190.8 0.8 add_select_fusion
  191.6 1.0 convert_reduce_fusion
  192.6 0.7 convert_reduce_fusion.1
  193.4 0.7 reshape.184
  194.0 1.8 select_reduce_fusion
  195.9 1.0 copy.49
  196.9 0.8 copy.50
  197.7 0.8 copy.51
  198.6 39.7 %all-to-all-done = bf16[16,24,2560]{2,1,0:T(8,128)(2,1)} async-done(((bf16[16,24,2560]{2,1,0:T(8,128)(2,1)}), bf16[16,24,2560]{2,1,0:T(8,128)(2,1)}, u32[]{:S(2)}, u32[]{:S(2)}) %all-to-all-start) | async-done | bytes 1966112 | tf_op jit(solution)/shard_map/all_to_all | solution.py:73
  238.2 3.8 %fusion.1 = bf16[256,2560]{1,0:T(8,128)(2,1)} fusion(bf16[384,2560]{1,0:T(8,128)(2,1)} %bitcast.18, bf16[256,2560]{1,0:T(8,128)(2,1)} %param.17, s32[256,384]{1,0:T(8,128)S(1)} %copy-done.6), kind=kOutput, calls=%fused_computation.4 | convolution fusion | flops 505380864 | bytes 4980736 | tf_op jit(solution)/shard_map/dot_general | solution.py:89
  242.1 4.3 %copy.55 = bf16[1,2560,768]{2,1,0:T(8,128)(2,1)} copy(bf16[1,2560,768]{2,1,0:T(8,128)(2,1)} %bitcast.95) | data formatting | bytes 7864320
  (30 shorter events, 1.1 us)
Async XLA Ops:
  7.2 17.5 %copy-start = (bf16[1,384,2560]{2,1,0:T(8,128)(2,1)S(1)}, bf16[1,384,2560]{2,1,0:T(8,128)(2,1)}, u32[]{:S(2)}) copy-start(bf16[1,384,2560]{2,1,0:T(8,128)(2,1)} %param.19) | copy-start | bytes 5898244
  7.2 108.2 %reduce-scatter.4.cloned.1.call-start = ((), (), s32[]{:S(2)}) async-start(), calls=%async_computation.5 | async-start | bytes 8355840
  23.8 0.8 copy-start.1
  39.0 1.0 copy-start.3
  39.0 1.1 copy-start.8
  39.0 134.1 %all-gather.3.cloned.1.call-start = ((), (), s32[]{:S(2)}) async-start(), calls=%async_computation.3 | async-start | bytes 8355840 | tf_op jit(solution)/shard_map/all_gather | solution.py:61
  40.1 1.2 copy-start.7
  40.9 201.1 %all-gather.5.cloned.1.call-start = ((), (), s32[]{:S(2)}) async-start(), calls=%async_computation.4 | async-start | bytes 4177920 | tf_op jit(solution)/shard_map/all_gather | solution.py:84
  120.6 52.5 %copy-start.2 = (bf16[1,384,768]{2,1,0:T(8,128)(2,1)S(1)}, bf16[1,384,768]{2,1,0:T(8,128)(2,1)}, u32[]{:S(2)}) copy-start(bf16[1,384,768]{2,1,0:T(8,128)(2,1)} %copy-done.1) | copy-start | bytes 1769476
  125.2 55.9 %all-to-all-start.1 = ((bf16[16,24,1]{1,2,0:T(2,128)(2,1)}), bf16[16,24,1]{1,2,0:T(2,128)(2,1)S(1)}, u32[]{:S(2)}, u32[]{:S(2)}) async-start(bf16[16,24,1]{1,2,0:T(2,128)(2,1)} %convert_element_type.135), calls=%async_computation.1 | async-start | bytes 16384 | tf_op jit(solution)/shard_map/all_to_all | solution.py:74
  181.0 0.6 copy-start.9
  181.0 9.8 %copy-start.10 = (s32[256,6]{0,1:T(8,128)S(1)}, s32[256,6]{0,1:T(8,128)}, u32[]{:S(2)}) copy-start(s32[256,6]{0,1:T(8,128)} %param.16) | copy-start | bytes 18436
  181.6 56.6 %all-to-all-start = ((bf16[16,24,2560]{2,1,0:T(8,128)(2,1)}), bf16[16,24,2560]{2,1,0:T(8,128)(2,1)}, u32[]{:S(2)}, u32[]{:S(2)}) async-start(bf16[16,24,2560]{2,1,0:T(8,128)(2,1)} %bitcast.97), calls=%async_computation | async-start | bytes 3932160 | tf_op jit(solution)/shard_map/all_to_all | solution.py:73
  190.8 6.1 %copy-start.5 = (bf16[1,160,768]{1,2,0:T(8,128)(2,1)S(1)}, bf16[1,160,768]{1,2,0:T(8,128)(2,1)}, u32[]{:S(2)}) copy-start(bf16[1,160,768]{1,2,0:T(8,128)(2,1)} %get-tuple-element.47) | copy-start | bytes 737284
  190.8 6.9 %copy-start.4 = (bf16[1,160,768]{1,2,0:T(8,128)(2,1)S(1)}, bf16[1,160,768]{1,2,0:T(8,128)(2,1)}, u32[]{:S(2)}) copy-start(bf16[1,160,768]{1,2,0:T(8,128)(2,1)} %get-tuple-element.46) | copy-start | bytes 737284
  196.9 41.4 %copy-start.6 = (s32[256,384]{1,0:T(8,128)S(1)}, s32[256,384]{1,0:T(8,128)}, u32[]{:S(2)}) copy-start(s32[256,384]{1,0:T(8,128)} %convert_reduce_fusion) | copy-start | bytes 1179652
Sparse Core Ops, SparseCore 0:
  39.1 76.2 reduce-scatter.3
  117.8 55.2 all-gather.2
  174.9 41.9 all-gather.4
where the time goes:
time: 255 us; the launch traced here: 253 us
  waiting for transfers between devices  150 us (59%)
  local copies, waits for them, and re-layouts  28.9 us (11%)
  other arithmetic  24.8 us (10%)
  starting transfers between devices  18.4 us (7%)
  matrix products  17 us (7%)
  between operations  13.8 us (5%)
    unnamed x4, waiting for transfers between devices  71.4 us
    all_to_all x1, waiting for transfers between devices, per_device(): lax.all_to_all(slot_grad, 'ep', split_axis=0, concat_axis=0, tiled=True)  39.7 us
    all_gather x1, waiting for transfers between devices, per_device(): lax.all_gather(weights_both, 'dp', axis=1, tiled=True)  38.8 us
    unnamed x31, local copies, waits for them, and re-layouts  23.7 us
    lt x1, other arithmetic, per_device(): position % capacity  10.9 us
    all_to_all x1, starting transfers between devices, per_device(): lax.all_to_all(slot_grad, 'ep', split_axis=0, concat_axis=0, tiled=True)  9.14 us
    all_to_all x1, starting transfers between devices, per_device(): lax.all_to_all(slot_score, 'ep', split_axis=0, concat_axis=0, tiled=True)  9.09 us
    dot_general x1, matrix products, per_device(): jnp.einsum('krh,knh->rn', grads_both, lax.all_gather(weights_both, 'dp',...  7.95 us
  transfers between devices with their start and end apart: 5, of which 3 were waited for; matrix products, arithmetic and copies ran while one was open for 13% of the time, Pallas kernels for 0%

commit v1 on v0

v1 whole, which is shorter than its diff:
```python
import jax
import jax.numpy as jnp
from jax import lax
from jax.experimental import pallas as pl
from jax.experimental.pallas import tpu as pltpu
from jax.sharding import PartitionSpec as P

first_decay = 0.9
second_decay = 0.95
learn_rate = 0.001
weight_decay = 0.1
adam_eps = 1e-08
first_fix = 1.0 - 0.9**10
second_fix = 1.0 - 0.95**10

D = 2560
H = 768
CAP = 24
EP = 16
DP = 16
ROWS = EP * CAP
TOK = 256
TOP = 6
BLK = D // DP
CHUNK = 640
NCH = D // CHUNK
MESH = pl.DeviceIdType.MESH
F32 = jnp.float32
BF16 = jnp.bfloat16


def kernel(
    re_h, rs_h, sh_h, cnt_h, xin_h, g_h, u_h, e_h, prob_h, mst_h, fst_h, snd_h, up_h,
    gi_o, sc_o, nm_o, nf_o, ns_o, nw_o,
    re, rs, cnt, prob, xin, g_in, u_in, e_in, mst, fst, snd, shared,
    w_all, dgate, dup, sc_row, sc_tile, sc_recv, comb,
    tmp, keep, r1_send, r1_recv, r2_send, r2_recv, r3_send, r3_recv, total,
    sg, rg, gi_v, sc_v, nm_v, nf_v, ns_v, nw_v,
    in_sem, out_sem, ag_s, ag_r, a2_s, a2_r, sc_s, sc_r, r1_s, r1_r, r2_s, r2_r, r3_s, r3_r,
    ng_s, ng_r,
):
    ep = lax.axis_index("ep")
    dp = lax.axis_index("dp")
    y, x, k = dp // 8, lax.rem(dp // 2, 4), lax.rem(dp, 2)

    def at(yy, xx, kk):
        return yy * 8 + lax.rem(xx + 4, 4) * 2 + kk

    sib, yp, xr, xl, x2 = at(y, x, 1 - k), at(1 - y, x, k), at(y, x + 1, k), at(y, x - 1, k), at(y, x + 2, k)

    def remote(src, dst, s, r, dst_dp):
        return pltpu.make_async_remote_copy(
            src_ref=src, dst_ref=dst, send_sem=s, recv_sem=r,
            device_id=(ep, dst_dp), device_id_type=MESH)

    loads = []

    def load(src, dst):
        c = pltpu.make_async_copy(src, dst, in_sem.at[len(loads)])
        c.start()
        loads.append(c)
        return c

    l_mst = load(mst_h.at[0], mst)
    l_up = load(up_h.at[0], w_all.at[dp, 1])
    l_g = load(g_h.at[0], g_in)
    l_u = load(u_h.at[0], u_in)
    l_e = load(e_h.at[0], e_in)
    l_cnt = load(cnt_h, cnt)
    l_prob = load(prob_h, prob)
    l_x = load(xin_h.at[0], xin)
    l_re = load(re_h, re)
    l_rs = load(rs_h, rs)
    l_sh = load(sh_h, shared)
    l_f = load(fst_h.at[0], fst)
    l_s = load(snd_h.at[0], snd)

    bar = pltpu.get_barrier_semaphore()
    for peer in (sib, yp, xr, xl, x2):
        pl.semaphore_signal(bar, inc=1, device_id=(ep, peer), device_id_type=MESH)

    def greet(i, _):
        pl.semaphore_signal(bar, inc=1, device_id=(lax.rem(ep + i, EP), dp), device_id_type=MESH)
        return _

    lax.fori_loop(1, EP, greet, 0)

    l_mst.wait()
    for r in range(0, BLK, 32):
        w_all[dp, 0, pl.ds(r, 32), :] = mst[pl.ds(r, 32), :].astype(BF16)
    l_up.wait()
    pl.semaphore_wait(bar, 5 + EP - 1)

    def ag(op, slot, half, to):
        ref = w_all.at[slot] if half is None else w_all.at[slot, half]
        return remote(ref, ref, ag_s.at[op], ag_r.at[op], to)

    plan = {
        0: (dp, None, sib), 1: (dp, None, yp), 2: (dp, None, xr), 3: (dp, None, xl),
        4: (xl, 0, xr), 5: (xl, None, sib), 6: (xr, 1, xl), 7: (xr, None, sib),
        8: (yp, None, xr), 9: (yp, None, xl), 10: (yp, None, sib),
        11: (at(1 - y, x - 1, k), 0, xr), 12: (at(1 - y, x - 1, k), None, sib),
        13: (at(1 - y, x + 1, k), 1, xl), 14: (at(1 - y, x + 1, k), None, sib),
        15: (x2, None, sib), 16: (at(1 - y, x + 2, k), None, sib),
    }
    def ag_go(*ops):
        for op in ops:
            ag(op, *plan[op]).start()

    def ag_wait(*ops):
        for op in ops:
            half = plan[op][1]
            ref = w_all.at[dp] if half is None else w_all.at[dp, half]
            remote(ref, ref, ag_s.at[op], ag_r.at[op], sib).wait_recv()

    ag_go(2, 3, 1, 0)

    l_g.wait()
    l_u.wait()
    l_e.wait()
    l_cnt.wait()
    l_prob.wait()
    TILE = 2 * CAP

    def hidden(i, carry):
        rows = pl.ds(pl.multiple_of(i * TILE, TILE), TILE)
        gv = g_in[rows, :].astype(F32)
        uv = u_in[rows, :].astype(F32)
        ev = e_in[rows, :].astype(F32)
        row = lax.broadcasted_iota(jnp.int32, (TILE, ROWS), 0) + i * TILE
        lane = lax.broadcasted_iota(jnp.int32, (TILE, ROWS), 1)
        p = jnp.sum(jnp.where(row == lane, prob[...], 0.0), axis=1, keepdims=True)
        row16 = lax.broadcasted_iota(jnp.int32, (TILE, EP), 0)
        second = (row16 >= CAP).astype(jnp.int32)
        block16 = second + 2 * i
        lane16 = lax.broadcasted_iota(jnp.int32, (TILE, EP), 1)
        limit = jnp.sum(jnp.where(block16 == lane16, cnt[...], 0), axis=1, keepdims=True)
        rank = (row16 - CAP * second)[:, :1]
        live = rank < limit
        sg_ = jax.nn.sigmoid(gv)
        act = gv * sg_
        score = jnp.sum(ev * act * uv, axis=1, keepdims=True)
        pe = p * ev
        d_up = (pe * act).astype(BF16)
        d_gate = (pe * uv * sg_ * (1.0 + gv * (1.0 - sg_))).astype(BF16)
        zero = jnp.zeros_like(d_up)
        dup[rows, :] = jnp.where(live, d_up, zero)
        dgate[rows, :] = jnp.where(live, d_gate, zero)
        score = score.astype(BF16).astype(F32)
        lane128 = lax.broadcasted_iota(jnp.int32, (TILE, 128), 1)
        spread = jnp.where(lane128 == rank, score, 0.0)
        sc_row[pl.ds(2 * i, 1), :] = jnp.sum(spread[:CAP], axis=0, keepdims=True)
        sc_row[pl.ds(2 * i + 1, 1), :] = jnp.sum(spread[CAP:], axis=0, keepdims=True)
        return carry

    lax.fori_loop(0, ROWS // TILE, hidden, 0)
    sc_tile[...] = sc_row[...].astype(BF16)

    def sc_copy(i):
        to = lax.rem(ep + i, EP)
        return pltpu.make_async_remote_copy(
            src_ref=sc_tile, dst_ref=sc_recv.at[ep], send_sem=sc_s.at[i], recv_sem=sc_r.at[i],
            device_id=(to, dp), device_id_type=MESH)

    sc_recv[ep] = sc_tile[...]

    l_x.wait()

    def r1_copy(c):
        blocks = pl.ds(pl.multiple_of(2 * c, 2), 2)
        return remote(r1_send.at[blocks], r1_recv.at[blocks], r1_s.at[c], r1_r.at[c], sib)

    def weight_part(i, carry):
        c = lax.rem(2 * (1 - y) + i, NCH)
        cols = pl.ds(pl.multiple_of(c * CHUNK, CHUNK), CHUNK)
        part = lax.dot_general(
            xin[:, cols], dgate[...], (((0,), (0,)), ((), ())), preferred_element_type=F32)
        tmp[...] = part.reshape(4, BLK, H)
        for j in range(2):
            keep[2 * c + j] = tmp[2 * j + k]
            r1_send[2 * c + j] = tmp[2 * j + 1 - k]
        r1_copy(c).start()
        return carry

    lax.fori_loop(0, NCH, weight_part, 0)

    def a2_copy(i, n):
        to = lax.rem(ep + n, EP)
        return pltpu.make_async_remote_copy(
            src_ref=sg.at[i, to], dst_ref=rg.at[i, ep], send_sem=a2_s.at[i, n], recv_sem=a2_r.at[i, n],
            device_id=(to, dp), device_id_type=MESH)

    pair = x // 2
    order = (2 * y + pair, 2 * y + 1 - pair, 2 * (1 - y) + pair, 2 * (1 - y) + 1 - pair)

    def rows_out(i):
        q = order[i]
        blocks = pl.ds(pl.multiple_of(4 * q, 4), 4)
        dims = (((1,), (1,)), ((), ()))
        wg = w_all[blocks, 0].reshape(CHUNK, H)
        wu = w_all[blocks, 1].reshape(CHUNK, H)
        out = lax.dot_general(dgate[...], wg, dims, preferred_element_type=F32)
        out = out + lax.dot_general(dup[...], wu, dims, preferred_element_type=F32)
        sg[i] = out.reshape(EP, CAP, CHUNK).astype(BF16)

        def send(n, carry):
            a2_copy(i, n).start()
            return carry

        lax.fori_loop(1, EP, send, 0)
        rg[i, ep] = sg[i, ep]

    ag_wait(2, 3)
    ag_go(4, 6, 5, 7)
    ag_wait(1)
    ag_go(8, 9, 10)
    ag_wait(0, 5, 7)
    rows_out(0)

    def send_scores(n, carry):
        sc_copy(n).start()
        return carry

    lax.fori_loop(1, EP, send_scores, 0)

    def r2_copy():
        return remote(r2_send, r2_recv, r2_s, r2_r, yp)

    def r1_wait(i, carry):
        c = lax.rem(2 * (1 - y) + i, NCH)
        r1_copy(c).wait_recv()
        return carry

    lax.fori_loop(0, 2, r1_wait, 0)

    def to_partner(n, carry):
        c = 4 * (1 - y) + n
        r2_send[n] = (keep[c] + r1_recv[c]).astype(BF16)
        return carry

    lax.fori_loop(0, 4, to_partner, 0)
    r2_copy().start()

    ag_wait(4, 6)
    ag_go(15)
    ag_wait(15)
    rows_out(1)

    ag_wait(8, 9)
    ag_go(11, 13, 12, 14)
    ag_wait(10, 12, 14)
    rows_out(2)

    lax.fori_loop(2, 4, r1_wait, 0)
    r2_copy().wait_recv()

    def r3_copy(n, to):
        return remote(r3_send.at[n], r3_recv.at[n], r3_s.at[n], r3_r.at[n], to)

    hops = (xr, xl, x2)
    for n, dx in enumerate((1, 3, 2)):
        xx = lax.rem(x + dx, 4)
        c = 4 * y + xx
        r3_send[n] = (keep[c] + r1_recv[c] + r2_recv[xx].astype(F32)).astype(BF16)
        r3_copy(n, hops[n]).start()
    total[...] = keep[4 * y + x] + r1_recv[4 * y + x] + r2_recv[x].astype(F32)

    ag_wait(11, 13)
    ag_go(16)
    ag_wait(16)
    rows_out(3)

    l_f.wait()
    l_s.wait()
    for n in range(3):
        r3_copy(n, hops[n]).wait_recv()

    def adam(i, carry):
        rows = pl.ds(pl.multiple_of(i * 32, 32), 32)
        wg = total[rows, :]
        for n in range(3):
            wg = wg + r3_recv[n, rows, :].astype(F32)
        m1 = first_decay * fst[rows, :].astype(F32) + (1.0 - first_decay) * wg
        m2 = second_decay * snd[rows, :].astype(F32) + (1.0 - second_decay) * wg * wg
        direction = m1 / first_fix / (jnp.sqrt(m2 / second_fix) + adam_eps)
        now = mst[rows, :]
        new = now - learn_rate * (direction + weight_decay * now)
        nm_v[rows, :] = new
        nf_v[rows, :] = m1.astype(BF16)
        ns_v[rows, :] = m2.astype(BF16)
        nw_v[rows, :] = new.astype(BF16)
        return carry

    lax.fori_loop(0, BLK // 32, adam, 0)

    outs = []

    def store(src, dst):
        c = pltpu.make_async_copy(src, dst, out_sem.at[len(outs)])
        c.start()
        outs.append(c)

    def nw_ref(slot, half=None):
        if half is None:
            return nw_o.at[0, pl.ds(pl.multiple_of(slot * BLK, BLK), BLK)]
        return nw_o.at[0, pl.ds(pl.multiple_of(slot * BLK + half * (BLK // 2), BLK // 2), BLK // 2)]

    def ng(op):
        slot, half, to = plan[op]
        ref = nw_ref(slot, half)
        return remote(nw_v if op < 4 else ref, ref, ng_s.at[op], ng_r.at[op], to)

    def ng_go(*ops):
        for op in ops:
            ng(op).start()

    def ng_wait(*ops):
        for op in ops:
            ng(op).wait_recv()

    ng_go(2, 3, 1, 0)
    store(nw_v, nw_ref(dp))
    store(nm_v, nm_o.at[0])
    store(nf_v, nf_o.at[0])
    store(ns_v, ns_o.at[0])

    l_re.wait()
    l_rs.wait()
    rank_of = rs[...]
    expert_of = re[...]
    served = (expert_of < EP) & (rank_of < CAP)
    target = jnp.where(served, expert_of * CAP + rank_of, -1)
    lane = lax.broadcasted_iota(jnp.int32, (TOK, ROWS), 1)
    hits = jnp.zeros((TOK, ROWS), F32)
    for j in range(TOP):
        hits = hits + jnp.where(target[:, j:j + 1] == lane, 1.0, 0.0)
    comb[...] = hits.astype(BF16)

    l_sh.wait()

    def tokens(i):
        def got(n, carry):
            a2_copy(i, n).wait_recv()
            return carry

        lax.fori_loop(1, EP, got, 0)
        rows = rg[i].astype(F32).reshape(ROWS, CHUNK).astype(BF16)
        routed = jnp.dot(comb[...], rows, preferred_element_type=F32)
        cols = pl.ds(pl.multiple_of(order[i] * CHUNK, CHUNK), CHUNK)
        gi_v[:, cols] = (shared[:, cols].astype(F32) + routed).astype(BF16)
        store(gi_v.at[:, cols], gi_o.at[:, cols])

    tokens(0)
    ng_wait(2, 3)
    ng_go(4, 6, 5, 7)
    ng_wait(1)
    ng_go(8, 9, 10)
    tokens(1)

    def got_score(n, carry):
        sc_copy(n).wait_recv()
        return carry

    lax.fori_loop(1, EP, got_score, 0)
    source = lax.broadcasted_iota(jnp.int32, (EP, EP, 128), 1)
    mine = jnp.sum(jnp.where(source == ep, sc_recv[...].astype(F32), 0.0), axis=1).astype(BF16)
    lane_e = lax.broadcasted_iota(jnp.int32, (TOK, EP), 1)
    lane_q = lax.broadcasted_iota(jnp.int32, (TOK, 128), 1)
    result = jnp.zeros((TOK, 128), F32)
    for j in range(TOP):
        pick = jnp.where(expert_of[:, j:j + 1] == lane_e, 1.0, 0.0).astype(BF16)
        scores = jnp.dot(pick, mine, preferred_element_type=F32)
        hit = (rank_of[:, j:j + 1] == lane_q) & served[:, j:j + 1]
        value = jnp.sum(jnp.where(hit, scores, 0.0), axis=1, keepdims=True)
        result = jnp.where(lane_q == j, value, result)
    sc_v[...] = result[:, :TOP].astype(BF16)
    store(sc_v, sc_o)

    ng_wait(4, 6)
    ng_go(15)
    ng_wait(8, 9)
    ng_go(11, 13, 12, 14)
    tokens(2)
    ng_wait(11, 13)
    ng_go(16)
    tokens(3)

    ng_wait(0, 5, 7, 10, 12, 14, 15, 16)
    for op in range(17):
        ag(op, *plan[op]).wait_send()
        ng(op).wait_send()

    def sent(n, carry):
        for i in range(NCH):
            a2_copy(i, n).wait_send()
        sc_copy(n).wait_send()
        return carry

    lax.fori_loop(1, EP, sent, 0)
    for c in range(NCH):
        r1_copy(c).wait_send()
    r2_copy().wait_send()
    for n in range(3):
        r3_copy(n, hops[n]).wait_send()
    for c in outs:
        c.wait()


def per_device(*args):
    any_spec = pl.BlockSpec(memory_space=pl.ANY)
    dma = pltpu.SemaphoreType.DMA
    V = pltpu.VMEM
    scratch = [
        V((TOK, TOP), jnp.int32), V((TOK, TOP), jnp.int32), V((1, EP), jnp.int32), V((1, ROWS), F32),
        V((ROWS, D), BF16), V((ROWS, H), BF16), V((ROWS, H), BF16), V((ROWS, H), BF16),
        V((BLK, H), F32), V((BLK, H), BF16), V((BLK, H), BF16), V((TOK, D), BF16),
        V((DP, 2, BLK, H), BF16), V((ROWS, H), BF16), V((ROWS, H), BF16),
        V((EP, 128), F32), V((EP, 128), BF16), V((EP, EP, 128), BF16), V((TOK, ROWS), BF16),
        V((4, BLK, H), F32), V((8, BLK, H), F32), V((8, BLK, H), F32), V((8, BLK, H), F32),
        V((4, BLK, H), BF16), V((4, BLK, H), BF16), V((3, BLK, H), BF16), V((3, BLK, H), BF16),
        V((BLK, H), F32),
        V((NCH, EP, CAP, CHUNK), BF16), V((NCH, EP, CAP, CHUNK), BF16),
        V((TOK, D), BF16), V((TOK, TOP), BF16), V((BLK, H), F32), V((BLK, H), BF16),
        V((BLK, H), BF16), V((BLK, H), BF16),
        dma((13,)), dma((9,)), dma((17,)), dma((17,)), dma((NCH, EP)), dma((NCH, EP)),
        dma((EP,)), dma((EP,)), dma((NCH,)), dma((NCH,)), dma, dma, dma((3,)), dma((3,)),
        dma((17,)), dma((17,)),
    ]
    return pl.pallas_call(
        kernel,
        out_shape=[
            jax.ShapeDtypeStruct((TOK, D), BF16), jax.ShapeDtypeStruct((TOK, TOP), BF16),
            jax.ShapeDtypeStruct((1, BLK, H), F32), jax.ShapeDtypeStruct((1, BLK, H), BF16),
            jax.ShapeDtypeStruct((1, BLK, H), BF16), jax.ShapeDtypeStruct((1, D, H), BF16),
        ],
        in_specs=[any_spec] * 13,
        out_specs=[any_spec] * 6,
        scratch_shapes=scratch,
        compiler_params=pltpu.CompilerParams(
            collective_id=0, has_side_effects=True, vmem_limit_bytes=60 * 2**20),
        name="backward_tail",
    )(*args)


def solution(mesh):
    in_specs = (
        P(("ep", "dp"), None),
        P(("ep", "dp"), None),
        P(("ep", "dp"), None),
        P("ep", "dp"),
        P("ep", "dp", None),
        P("ep", "dp", None),
        P("ep", "dp", None),
        P("ep", "dp", None),
        P("ep", "dp"),
        P("ep", "dp", None),
        P("ep", "dp", None),
        P("ep", "dp", None),
        P("ep", "dp", None),
    )
    out_specs = (
        P(("ep", "dp"), None),
        P(("ep", "dp"), None),
        P("ep", "dp", None),
        P("ep", "dp", None),
        P("ep", "dp", None),
        P("ep", None, None),
    )
    return jax.shard_map(
        per_device, mesh=mesh, in_specs=in_specs, out_specs=out_specs, check_vma=False
    )
```

time: 255 us -> 122 us (0.48)
  waiting for transfers between devices: 150 us -> 0 us
  Pallas kernels: 0 us -> 108 us
  other arithmetic: 24.8 us -> 0 us
  starting transfers between devices: 18.4 us -> 0 us
  matrix products: 17 us -> 0 us
  local copies, waits for them, and re-layouts: 28.9 us -> 13.2 us
  between operations: 13.8 us -> 0.65 us
    pallas_call x0 -> x1, Pallas kernels: none -> 108 us  [per_device(): pl.pallas_call(kernel, out_shape=[jax.ShapeDtypeStruct((TOK, D), BF16), j...]
    unnamed x4 -> x0, waiting for transfers between devices: 71.4 us -> none
    all_to_all x2 -> x0, waiting for transfers between devices: 39.7 us -> none  [the longest x1 39.7 us: per_device(): lax.all_to_all(slot_grad, 'ep', split_axis=0, concat_axis=0, tiled=True)]
    all_gather x2 -> x0, waiting for transfers between devices: 38.8 us -> none  [the longest x1 38.8 us: per_device(): lax.all_gather(weights_both, 'dp', axis=1, tiled=True)]
    all_to_all x2 -> x0, starting transfers between devices: 18.2 us -> none  [the longest x1 9.14 us: per_device(): lax.all_to_all(slot_grad, 'ep', split_axis=0, concat_axis=0, tiled=True)]
    dot_general x3 -> x0, matrix products: 17 us -> none  [the longest x1 7.95 us: per_device(): jnp.einsum('krh,knh->rn', grads_both, lax.all_gather(weights_both, 'dp',...]
    unnamed x31 -> x11, local copies, waits for them, and re-layouts: 23.7 us -> 11.6 us
    lt x1 -> x0, other arithmetic: 10.9 us -> none  [per_device(): position % capacity]
  transfers between devices with their start and end apart: 5 -> 0, of which waited for: 3 -> 0; matrix products, arithmetic and copies ran while one was open for 13% -> 0% of each run, Pallas kernels for 0% -> 0%
where the time goes in v1:
time: 122 us; the launch traced here: 121 us
  Pallas kernels  108 us (89%)
  local copies, waits for them, and re-layouts  13.2 us (11%)
    pallas_call x1, Pallas kernels, per_device(): pl.pallas_call(kernel, out_shape=[jax.ShapeDtypeStruct((TOK, D), BF16), j...  108 us
    unnamed x11, local copies, waits for them, and re-layouts  11.6 us

profile of v1, /device:TPU:1, one launch (start us, length us, event | category | flops | bytes accessed | tf_op | source)
XLA Modules:
  0.0 121.4 jit_solution(3959319602199749050)
XLA Ops:
  0.6 1.5 %copy.19.re_h = s32[256,6]{1,0:T(8,128)} copy(s32[256,6]{0,1:T(8,128)} %param.13) | data formatting | bytes 12288 | tf_op args[0]
  2.1 1.5 %copy.20.rs_h = s32[256,6]{1,0:T(8,128)} copy(s32[256,6]{0,1:T(8,128)} %param.14) | data formatting | bytes 12288 | tf_op args[1]
  3.6 107.6 %backward_tail.1 = (bf16[256,2560]{1,0:T(8,128)(2,1)}, bf16[256,6]{1,0:T(8,128)(2,1)}, f32[1,160,768]{2,1,0:T(8,128)}, bf16[1,160,768]{2,1,0:T(8,128)(2,1)}, bf1...) custom-call(s32[256,6]{1,0:T(8,128)} %copy.19.re_h, s32[256,6]{1,0:T(8,128)} %copy.20.rs_h, ...), custom_call_target="tpu_custom_call" | custom-call | tf_op jit(solution)/shard_map/backward_tail/pallas_call | solution.py:429
  111.2 0.0 copy-start.1
  111.2 1.6 %copy.21 = bf16[256,6]{0,1:T(8,128)(2,1)} copy(bf16[256,6]{1,0:T(8,128)(2,1)} %get-tuple-element.7) | data formatting | bytes 6144 | tf_op jit(solution)/shard_map/backward_tail/pallas_call | solution.py:429
  112.8 0.0 copy-start
  112.8 2.6 %copy.27 = bf16[256,2560]{1,0:T(8,128)(2,1)} copy(bf16[256,2560]{1,0:T(8,128)(2,1)} %get-tuple-element.18) | data formatting | bytes 2621440
  115.4 0.0 copy-done.1
  115.4 0.8 copy.28
  116.2 1.7 %copy.29 = bf16[1,160,768]{2,1,0:T(8,128)(2,1)} copy(bf16[1,160,768]{2,1,0:T(8,128)(2,1)} %get-tuple-element.21) | data formatting | bytes 491520
  117.8 1.7 %copy.30 = bf16[1,160,768]{2,1,0:T(8,128)(2,1)} copy(bf16[1,160,768]{2,1,0:T(8,128)(2,1)} %get-tuple-element.22) | data formatting | bytes 491520
  119.5 0.0 copy-done
  119.5 1.9 %copy.31 = bf16[1,2560,768]{2,1,0:T(8,128)(2,1)} copy(bf16[1,2560,768]{2,1,0:T(8,128)(2,1)S(1)} %copy-done) | data formatting | bytes 7864320
Async XLA Ops:
  111.2 4.2 %copy-start.1 = (f32[1,160,768]{2,1,0:T(8,128)S(1)}, f32[1,160,768]{2,1,0:T(8,128)}, u32[]{:S(2)}) copy-start(f32[1,160,768]{2,1,0:T(8,128)} %get-tuple-element.20) | copy-start | bytes 1474564
  112.8 6.7 %copy-start = (bf16[1,2560,768]{2,1,0:T(8,128)(2,1)S(1)}, bf16[1,2560,768]{2,1,0:T(8,128)(2,1)}, u32[]{:S(2)}) copy-start(bf16[1,2560,768]{2,1,0:T(8,128)(2,1)} %get-tuple-element.23) | copy-start | bytes 11796484

commit v2 on v1

v2 whole, which is shorter than its diff:
```python
import jax
import jax.numpy as jnp
from jax import lax
from jax.experimental import pallas as pl
from jax.experimental.pallas import tpu as pltpu
from jax.sharding import PartitionSpec as P

first_decay = 0.9
second_decay = 0.95
learn_rate = 0.001
weight_decay = 0.1
adam_eps = 1e-08
first_fix = 1.0 - 0.9**10
second_fix = 1.0 - 0.95**10

D = 2560
H = 768
CAP = 24
EP = 16
DP = 16
ROWS = EP * CAP
TOK = 256
TOP = 6
BLK = D // DP
CHUNK = 640
NCH = D // CHUNK
MESH = pl.DeviceIdType.MESH
F32 = jnp.float32
BF16 = jnp.bfloat16


PIECES = ((0, 80), (80, 80))
NQ = len(PIECES)


def kernel(
    re_h, rs_h, sh_h, cnt_h, xin_h, g_h, u_h, e_h, prob_h, mst_h, fst_h, snd_h, up_h,
    gi_o, sc_o, nm_o, nf_o, ns_o, nw_o,
    re, rs, cnt, prob, xin, g_in, u_in, e_in, mst, fst, snd, shared,
    w_gate, w_up, dgate, dup, sc_row, sc_tile, sc_recv, comb,
    tmp, keep, r1_send, r1_recv, r2_send, r2_recv, r3_send, r3_recv,
    sg_a, rg_a, sg_b, rg_b, sg, rg, gi_v, sc_v, nm_v, nf_v, ns_v, nw_v,
    in_sem, out_sem, ag_s, ag_r, a2_s, a2_r, sc_s, sc_r, r1_s, r1_r, r2_s, r2_r, r3_s, r3_r,
    ng_s, ng_r,
):
    ep = lax.axis_index("ep")
    dp = lax.axis_index("dp")
    y, x, k = dp // 8, lax.rem(dp // 2, 4), lax.rem(dp, 2)

    def at(yy, xx, kk):
        return yy * 8 + lax.rem(xx + 4, 4) * 2 + kk

    sib, yp, xr, xl, x2 = at(y, x, 1 - k), at(1 - y, x, k), at(y, x + 1, k), at(y, x - 1, k), at(y, x + 2, k)
    yxr, yxl, yx2 = at(1 - y, x + 1, k), at(1 - y, x - 1, k), at(1 - y, x + 2, k)

    def remote(src, dst, s, r, dst_dp):
        return pltpu.make_async_remote_copy(
            src_ref=src, dst_ref=dst, send_sem=s, recv_sem=r,
            device_id=(ep, dst_dp), device_id_type=MESH)

    def rows_of(slot, q=None):
        if q is None:
            return pl.ds(pl.multiple_of(slot * BLK, BLK), BLK)
        return pl.ds(pl.multiple_of(slot * BLK + PIECES[q][0], 16), PIECES[q][1])

    loads = []

    def load(src, dst):
        c = pltpu.make_async_copy(src, dst, in_sem.at[len(loads)])
        c.start()
        loads.append(c)
        return c

    l_mst = load(mst_h.at[0], mst)
    l_up = load(up_h.at[0], w_up.at[rows_of(dp)])
    l_g = load(g_h.at[0], g_in)
    l_u = load(u_h.at[0], u_in)
    l_e = load(e_h.at[0], e_in)
    l_cnt = load(cnt_h, cnt)
    l_prob = load(prob_h, prob)
    l_x = load(xin_h.at[0], xin)
    l_re = load(re_h, re)
    l_rs = load(rs_h, rs)
    l_f = load(fst_h.at[0], fst)
    l_s = load(snd_h.at[0], snd)
    l_sh = load(sh_h, shared)

    bar = pltpu.get_barrier_semaphore()
    for peer in (sib, yp, xr, xl, x2):
        pl.semaphore_signal(bar, inc=1, device_id=(ep, peer), device_id_type=MESH)

    def greet(i, _):
        pl.semaphore_signal(bar, inc=1, device_id=(lax.rem(ep + i, EP), dp), device_id_type=MESH)
        return _

    lax.fori_loop(1, EP, greet, 0)

    l_mst.wait()
    for r in range(0, BLK, 32):
        w_gate[pl.ds(pl.multiple_of(dp * BLK + r, 32), 32), :] = mst[pl.ds(r, 32), :].astype(BF16)
    l_up.wait()
    pl.semaphore_wait(bar, 5 + EP - 1)

    plan = (
        (dp, 0, xr), (dp, 1, xr), (dp, 1, xl), (dp, 0, xl),
        (dp, 0, yp), (dp, 1, yp), (dp, 0, sib), (dp, 1, sib),
        (xl, 0, xr), (xr, 1, xl),
        (xl, 0, sib), (xl, 1, sib), (xr, 0, sib), (xr, 1, sib),
        (yp, 0, xr), (yp, 0, xl), (yp, 1, xr), (yp, 1, xl), (yp, 0, sib), (yp, 1, sib),
        (yxl, 0, xr), (yxr, 1, xl),
        (yxl, 0, sib), (yxl, 1, sib), (yxr, 0, sib), (yxr, 1, sib),
        (x2, 0, sib), (x2, 1, sib), (yx2, 0, sib), (yx2, 1, sib),
    )

    def ag(op):
        slot, piece, to = plan[op]
        ref = (w_gate, w_up)[piece].at[rows_of(slot)]
        return remote(ref, ref, ag_s.at[op], ag_r.at[op], to)

    def ag_go(*ops):
        for op in ops:
            ag(op).start()

    def ag_wait(*ops):
        for op in ops:
            ag(op).wait_recv()

    ag_go(0, 2, 4, 1, 3, 5, 6, 7)

    l_g.wait()
    l_u.wait()
    l_e.wait()
    l_cnt.wait()
    l_prob.wait()
    TILE = 2 * CAP

    def hidden(i, carry):
        rows = pl.ds(pl.multiple_of(i * TILE, TILE), TILE)
        gv = g_in[rows, :].astype(F32)
        uv = u_in[rows, :].astype(F32)
        ev = e_in[rows, :].astype(F32)
        row = lax.broadcasted_iota(jnp.int32, (TILE, ROWS), 0) + i * TILE
        lane = lax.broadcasted_iota(jnp.int32, (TILE, ROWS), 1)
        p = jnp.sum(jnp.where(row == lane, prob[...], 0.0), axis=1, keepdims=True)
        row16 = lax.broadcasted_iota(jnp.int32, (TILE, EP), 0)
        second = (row16 >= CAP).astype(jnp.int32)
        block16 = second + 2 * i
        lane16 = lax.broadcasted_iota(jnp.int32, (TILE, EP), 1)
        limit = jnp.sum(jnp.where(block16 == lane16, cnt[...], 0), axis=1, keepdims=True)
        rank = (row16 - CAP * second)[:, :1]
        live = rank < limit
        sg_ = jax.nn.sigmoid(gv)
        act = gv * sg_
        score = jnp.sum(ev * act * uv, axis=1, keepdims=True)
        pe = p * ev
        d_up = (pe * act).astype(BF16)
        d_gate = (pe * uv * sg_ * (1.0 + gv * (1.0 - sg_))).astype(BF16)
        zero = jnp.zeros_like(d_up)
        dup[rows, :] = jnp.where(live, d_up, zero)
        dgate[rows, :] = jnp.where(live, d_gate, zero)
        score = score.astype(BF16).astype(F32)
        lane128 = lax.broadcasted_iota(jnp.int32, (TILE, 128), 1)
        spread = jnp.where(lane128 == rank, score, 0.0)
        sc_row[pl.ds(2 * i, 1), :] = jnp.sum(spread[:CAP], axis=0, keepdims=True)
        sc_row[pl.ds(2 * i + 1, 1), :] = jnp.sum(spread[CAP:], axis=0, keepdims=True)
        return carry

    lax.fori_loop(0, ROWS // TILE, hidden, 0)
    sc_tile[...] = sc_row[...].astype(BF16)

    def sc_copy(i):
        to = lax.rem(ep + i, EP)
        return pltpu.make_async_remote_copy(
            src_ref=sc_tile, dst_ref=sc_recv.at[ep], send_sem=sc_s.at[i], recv_sem=sc_r.at[i],
            device_id=(to, dp), device_id_type=MESH)

    sc_recv[ep] = sc_tile[...]

    pair, odd = x // 2, lax.rem(x, 2)
    base = CHUNK * (2 * y + pair)
    groups = (
        (sg_a, rg_a, base + odd * 384, 256),
        (sg_b, rg_b, base + (1 - odd) * 256, 384),
        (sg.at[0], rg.at[0], CHUNK * (2 * y + 1 - pair), CHUNK),
        (sg.at[1], rg.at[1], CHUNK * (2 * (1 - y) + pair), CHUNK),
        (sg.at[2], rg.at[2], CHUNK * (2 * (1 - y) + 1 - pair), CHUNK),
    )

    def a2_copy(i, n):
        to = lax.rem(ep + n, EP)
        src, dst = groups[i][:2]
        return pltpu.make_async_remote_copy(
            src_ref=src.at[to], dst_ref=dst.at[ep], send_sem=a2_s.at[i, n], recv_sem=a2_r.at[i, n],
            device_id=(to, dp), device_id_type=MESH)

    def rows_send(i, first, last, odd_step):
        def send(n, carry):
            a2_copy(i, 2 * n + odd_step).start()
            return carry

        lax.fori_loop(first, last, send, 0)

    def rows_out(i, later=False):
        src, dst, col, width = groups[i]
        rows = pl.ds(pl.multiple_of(col, 128), width)
        dims = (((1,), (1,)), ((), ()))
        out = lax.dot_general(dgate[...], w_gate[rows, :], dims, preferred_element_type=F32)
        out = out + lax.dot_general(dup[...], w_up[rows, :], dims, preferred_element_type=F32)
        src[...] = out.reshape(EP, CAP, width).astype(BF16)

        dst[ep] = src[ep]
        rows_send(i, 1, EP // 2, 0)
        if not later:
            rows_send(i, 0, EP // 2, 1)

    l_x.wait()

    def r1_copy(c):
        blocks = pl.ds(pl.multiple_of(2 * c, 2), 2)
        return remote(r1_send.at[blocks], r1_recv.at[blocks], r1_s.at[c], r1_r.at[c], sib)

    def weight_part(i, carry):
        c = lax.rem(2 * (1 - y) + i, NCH)
        cols = pl.ds(pl.multiple_of(c * CHUNK, CHUNK), CHUNK)
        part = lax.dot_general(
            xin[:, cols], dgate[...], (((0,), (0,)), ((), ())), preferred_element_type=F32)
        tmp[...] = part.reshape(4, BLK, H)
        for j in range(2):
            keep[2 * c + j] = tmp[2 * j + k]
            r1_send[2 * c + j] = tmp[2 * j + 1 - k]
        r1_copy(c).start()
        return carry

    def r1_wait(i, carry):
        c = lax.rem(2 * (1 - y) + i, NCH)
        r1_copy(c).wait_recv()
        return carry

    def piece_of(q):
        return pl.ds(*PIECES[q])

    def r2_copy(q):
        rows = piece_of(q)
        return remote(r2_send.at[:, rows], r2_recv.at[:, rows], r2_s.at[q], r2_r.at[q], yp)

    lax.fori_loop(0, 2, weight_part, 0)
    ag_wait(6, 7)
    rows_out(0, later=True)
    lax.fori_loop(2, NCH, weight_part, 0)
    ag_wait(0, 2)
    ag_go(8, 9, 10, 13)
    ag_wait(4)
    ag_go(14, 15, 18)

    lax.fori_loop(0, 2, r1_wait, 0)
    for q in range(NQ):
        rows = piece_of(q)

        def to_partner(n, carry):
            c = 4 * (1 - y) + n
            r2_send[n, rows] = (keep[c, rows] + r1_recv[c, rows]).astype(BF16)
            return carry

        lax.fori_loop(0, 4, to_partner, 0)
        r2_copy(q).start()

    def send_scores(n, carry):
        sc_copy(n).start()
        return carry

    lax.fori_loop(1, EP, send_scores, 0)

    l_re.wait()
    l_rs.wait()
    rank_of = rs[...]
    expert_of = re[...]
    served = (expert_of < EP) & (rank_of < CAP)
    target = jnp.where(served, expert_of * CAP + rank_of, -1)
    row_j = lax.broadcasted_iota(jnp.int32, (ROWS, TOK), 0)
    hits = jnp.zeros((ROWS, TOK), F32)
    for j in range(TOP):
        hits = hits + jnp.where(target[j:j + 1, :] == row_j, 1.0, 0.0)
    comb[...] = hits.T.astype(BF16)

    ag_wait(1, 3)
    ag_go(11, 12)
    ag_wait(5)
    ag_go(16, 17, 19)
    ag_wait(10, 11, 12, 13)
    rows_out(1, later=True)

    def r3_copy(n, q):
        rows = piece_of(q)
        return remote(r3_send.at[n, rows], r3_recv.at[n, rows], r3_s.at[n, q], r3_r.at[n, q],
                      (xr, xl, x2)[n])

    def over_x(q):
        r2_copy(q).wait_recv()
        rows = piece_of(q)
        for n, dx in enumerate((1, 3, 2)):
            xx = lax.rem(x + dx, 4)
            c = 4 * y + xx
            r3_send[n, rows] = (
                keep[c, rows] + r1_recv[c, rows] + r2_recv[xx, rows].astype(F32)
            ).astype(BF16)
            r3_copy(n, q).start()

    outs = []

    def store(src, dst):
        c = pltpu.make_async_copy(src, dst, out_sem.at[len(outs)])
        c.start()
        outs.append(c)

    ng_plan = (
        (dp, 0, xr), (dp, 0, xl), (dp, 0, yp), (dp, 0, sib),
        (xl, 0, xr), (xl, 0, sib), (xr, 0, sib),
        (yp, 0, xr), (yp, 0, xl), (yp, 0, sib),
        (yxr, 0, xl), (yxl, 0, sib), (yxr, 0, sib), (x2, 0, sib), (yx2, 0, sib),
        (dp, 1, xr), (dp, 1, xl), (dp, 1, yp), (dp, 1, sib),
        (xr, 1, xl), (xr, 1, yp), (xr, 1, sib), (xl, 1, yp), (xl, 1, sib),
        (x2, 1, yp), (x2, 1, sib), (yp, 1, sib), (yxr, 1, sib), (yxl, 1, sib), (yx2, 1, sib),
    )

    def ng(op):
        slot, q, to = ng_plan[op]
        ref = nw_o.at[0, rows_of(slot, q)]
        src = nw_v.at[piece_of(q)] if slot is dp else ref
        return remote(src, ref, ng_s.at[op], ng_r.at[op], to)

    def ng_go(*ops):
        for op in ops:
            ng(op).start()

    def ng_hop(*moves):
        for arrived, *onward in moves:
            ng(arrived).wait_recv()
            ng_go(*onward)

    def step(q):
        for n in range(3):
            r3_copy(n, q).wait_recv()
        first, size = PIECES[q]

        def adam(i, carry):
            rows = pl.ds(pl.multiple_of(first + i * 16, 16), 16)
            own = 4 * y + x
            wg = keep[own, rows] + r1_recv[own, rows] + r2_recv[x, rows].astype(F32)
            for n in range(3):
                wg = wg + r3_recv[n, rows].astype(F32)
            m1 = first_decay * fst[rows, :].astype(F32) + (1.0 - first_decay) * wg
            m2 = second_decay * snd[rows, :].astype(F32) + (1.0 - second_decay) * wg * wg
            direction = m1 / first_fix / (jnp.sqrt(m2 / second_fix) + adam_eps)
            now = mst[rows, :]
            new = now - learn_rate * (direction + weight_decay * now)
            nm_v[rows, :] = new
            nf_v[rows, :] = m1.astype(BF16)
            ns_v[rows, :] = m2.astype(BF16)
            nw_v[rows, :] = new.astype(BF16)
            return carry

        lax.fori_loop(0, size // 16, adam, 0)

    def tokens(i):
        _, got, col, width = groups[i]

        def arrived(n, carry):
            a2_copy(i, n).wait_recv()
            return carry

        lax.fori_loop(1, EP, arrived, 0)
        rows = got[...].astype(F32).reshape(ROWS, width).astype(BF16)
        routed = jnp.dot(comb[...], rows, preferred_element_type=F32)
        cols = pl.ds(pl.multiple_of(col, 128), width)
        gi_v[:, cols] = (shared[:, cols].astype(F32) + routed).astype(BF16)
        store(gi_v.at[:, cols], gi_o.at[:, cols])

    def scores_out():
        def got_score(n, carry):
            sc_copy(n).wait_recv()
            return carry

        lax.fori_loop(1, EP, got_score, 0)
        source = lax.broadcasted_iota(jnp.int32, (EP, EP, 128), 1)
        mine = jnp.sum(jnp.where(source == ep, sc_recv[...].astype(F32), 0.0), axis=1).astype(BF16)
        row_e = lax.broadcasted_iota(jnp.int32, (EP, TOK), 0)
        row_q = lax.broadcasted_iota(jnp.int32, (128, TOK), 0)
        row_k = lax.broadcasted_iota(jnp.int32, (8, TOK), 0)
        result = jnp.zeros((8, TOK), F32)
        for j in range(TOP):
            pick = jnp.where(expert_of[j:j + 1, :] == row_e, 1.0, 0.0).astype(BF16)
            scores = lax.dot_general(mine, pick, (((0,), (0,)), ((), ())), preferred_element_type=F32)
            hit = jnp.where(served[j:j + 1, :], rank_of[j:j + 1, :], -1) == row_q
            value = jnp.sum(jnp.where(hit, scores, 0.0), axis=0, keepdims=True)
            result = jnp.where(row_k == j, value, result)
        sc_v[...] = result[:TOP].astype(BF16)
        store(sc_v, sc_o)

    l_f.wait()
    l_s.wait()
    l_sh.wait()
    lax.fori_loop(2, NCH, r1_wait, 0)

    ag_wait(8, 9)
    ag_go(26, 27)
    ag_wait(26, 27)
    rows_out(2)
    ag_wait(14, 15)
    ag_go(20, 22, 24)
    over_x(0)
    ag_wait(16, 17)
    ag_go(21, 23, 25)
    ag_wait(18, 19, 22, 23, 24, 25)
    rows_out(3)
    rows_send(0, 0, EP // 2, 1)
    rows_send(1, 0, EP // 2, 1)
    scores_out()
    ag_wait(20, 21)
    ag_go(28, 29)
    over_x(1)
    ag_wait(28, 29)
    rows_out(4)
    step(0)
    ng_go(0, 1, 2, 3)
    step(1)
    ng_go(15, 16, 17, 18)
    ng_hop((0, 4, 5), (2, 7, 8, 9), (16, 19, 20, 21), (15, 22, 23), (1, 6))
    tokens(0)
    tokens(1)
    ng_hop((8, 10, 12), (19, 24, 25), (7, 11), (4, 13), (17, 26), (20, 27), (22, 28))
    store(nw_v, nw_o.at[0, rows_of(dp)])
    store(nm_v, nm_o.at[0])
    store(nf_v, nf_o.at[0])
    store(ns_v, ns_o.at[0])
    tokens(2)
    ng_hop((10, 14), (24, 29))
    tokens(3)
    tokens(4)
    ng_hop(*((op,) for op in (3, 5, 6, 9, 11, 12, 13, 14, 18, 21, 23, 25, 26, 27, 28, 29)))

    for op in range(len(plan)):
        ag(op).wait_send()
        ng(op).wait_send()

    def sent(n, carry):
        for i in range(len(groups)):
            a2_copy(i, n).wait_send()
        sc_copy(n).wait_send()
        return carry

    lax.fori_loop(1, EP, sent, 0)
    for c in range(NCH):
        r1_copy(c).wait_send()
    for q in range(NQ):
        r2_copy(q).wait_send()
        for n in range(3):
            r3_copy(n, q).wait_send()
    for c in outs:
        c.wait()


def finish(*refs):
    n = (len(refs) - 2) // 3
    srcs, dsts, held, in_sem, out_sem = refs[:n], refs[n:2 * n], refs[2 * n:3 * n], refs[-2], refs[-1]
    ins, outs = [], []
    for src, dst, mid in zip(srcs, dsts, held):
        rows = src.shape[-2]
        parts = 8 if rows == D else 4 if rows == TOK else 1
        for i in range(parts):
            part = pl.ds(i * (rows // parts), rows // parts)
            index = (0, part) if len(src.shape) == 3 else (part,)
            m = len(ins)
            ins.append(pltpu.make_async_copy(src.at[index], mid.at[index], in_sem.at[m]))
            outs.append(pltpu.make_async_copy(mid.at[index], dst.at[index], out_sem.at[m]))
    for c in ins:
        c.start()
    for c, o in zip(ins, outs):
        c.wait()
        o.start()
    for o in outs:
        o.wait()


def per_device(route_experts, route_slots, *args):
    any_spec = pl.BlockSpec(memory_space=pl.ANY)
    dma = pltpu.SemaphoreType.DMA
    V = pltpu.VMEM
    scratch = [
        V((TOP, TOK), jnp.int32), V((TOP, TOK), jnp.int32), V((1, EP), jnp.int32), V((1, ROWS), F32),
        V((ROWS, D), BF16), V((ROWS, H), BF16), V((ROWS, H), BF16), V((ROWS, H), BF16),
        V((BLK, H), F32), V((BLK, H), BF16), V((BLK, H), BF16), V((TOK, D), BF16),
        V((D, H), BF16), V((D, H), BF16), V((ROWS, H), BF16), V((ROWS, H), BF16),
        V((EP, 128), F32), V((EP, 128), BF16), V((EP, EP, 128), BF16), V((TOK, ROWS), BF16),
        V((4, BLK, H), F32), V((8, BLK, H), F32), V((8, BLK, H), F32), V((8, BLK, H), F32),
        V((4, BLK, H), BF16), V((4, BLK, H), BF16), V((3, BLK, H), BF16), V((3, BLK, H), BF16),
        V((EP, CAP, 256), BF16), V((EP, CAP, 256), BF16), V((EP, CAP, 384), BF16), V((EP, CAP, 384), BF16),
        V((3, EP, CAP, CHUNK), BF16), V((3, EP, CAP, CHUNK), BF16),
        V((TOK, D), BF16), V((TOP, TOK), BF16), V((BLK, H), F32), V((BLK, H), BF16),
        V((BLK, H), BF16), V((BLK, H), BF16),
        dma((13,)), dma((10,)), dma((30,)), dma((30,)), dma((5, EP)), dma((5, EP)),
        dma((EP,)), dma((EP,)), dma((NCH,)), dma((NCH,)), dma((NQ,)), dma((NQ,)), dma((3, NQ)), dma((3, NQ)),
        dma((30,)), dma((30,)),
    ]
    shapes = [
        jax.ShapeDtypeStruct((TOK, D), BF16), jax.ShapeDtypeStruct((TOP, TOK), BF16),
        jax.ShapeDtypeStruct((1, BLK, H), F32), jax.ShapeDtypeStruct((1, BLK, H), BF16),
        jax.ShapeDtypeStruct((1, BLK, H), BF16), jax.ShapeDtypeStruct((1, D, H), BF16),
    ]
    parts = pl.pallas_call(
        kernel,
        out_shape=shapes,
        in_specs=[any_spec] * 13,
        out_specs=[any_spec] * 6,
        scratch_shapes=scratch,
        compiler_params=pltpu.CompilerParams(
            collective_id=0, has_side_effects=True, vmem_limit_bytes=60 * 2**20),
        name="backward_tail",
    )(route_experts.T, route_slots.T, *args)
    grad, score, *rest = pl.pallas_call(
        finish,
        out_shape=shapes,
        in_specs=[any_spec] * 6,
        out_specs=[any_spec] * 6,
        scratch_shapes=[V(t.shape, t.dtype) for t in shapes] + [dma((16,)), dma((16,))],
        compiler_params=pltpu.CompilerParams(vmem_limit_bytes=60 * 2**20),
        name="finish",
    )(*parts)
    return (grad, score.T, *rest)


def solution(mesh):
    in_specs = (
        P(("ep", "dp"), None),
        P(("ep", "dp"), None),
        P(("ep", "dp"), None),
        P("ep", "dp"),
        P("ep", "dp", None),
        P("ep", "dp", None),
        P("ep", "dp", None),
        P("ep", "dp", None),
        P("ep", "dp"),
        P("ep", "dp", None),
        P("ep", "dp", None),
        P("ep", "dp", None),
        P("ep", "dp", None),
    )
    out_specs = (
        P(("ep", "dp"), None),
        P(("ep", "dp"), None),
        P("ep", "dp", None),
        P("ep", "dp", None),
        P("ep", "dp", None),
        P("ep", None, None),
    )
    return jax.shard_map(
        per_device, mesh=mesh, in_specs=in_specs, out_specs=out_specs, check_vma=False
    )
```

time: 122 us -> 90.8 us (0.74)
  Pallas kernels: 108 us -> 90.1 us
  local copies, waits for them, and re-layouts: 13.2 us -> 0 us
    pallas_call x1 -> x2, Pallas kernels: 108 us -> 90.1 us  [the longest x1 84.7 us: per_device(): pl.pallas_call(kernel, out_shape=shapes, in_specs=[any_spec] * 13, out_sp...]
    unnamed x11 -> x0, local copies, waits for them, and re-layouts: 11.6 us -> none
    pallas_call x1 -> x0, local copies, waits for them, and re-layouts: 1.58 us -> none  [per_device(): pl.pallas_call(kernel, out_shape=[jax.ShapeDtypeStruct((TOK, D), BF16), j...]
where the time goes in v2:
time: 90.8 us; the launch traced here: 90.7 us
  Pallas kernels  90.1 us (99%)
    pallas_call x1, Pallas kernels, per_device(): pl.pallas_call(kernel, out_shape=shapes, in_specs=[any_spec] * 13, out_sp...  84.7 us
    pallas_call x1, Pallas kernels, per_device(): pl.pallas_call(finish, out_shape=shapes, in_specs=[any_spec] * 6, out_spe...  5.36 us

profile of v2, /device:TPU:1, one launch (start us, length us, event | category | flops | bytes accessed | tf_op | source)
XLA Modules:
  0.0 90.7 jit_solution(10199343591097460686)
XLA Ops:
  0.6 84.7 %backward_tail.1 = (bf16[256,2560]{1,0:T(8,128)(2,1)}, bf16[6,256]{1,0:T(8,128)(2,1)}, f32[1,160,768]{2,1,0:T(8,128)}, bf16[1,160,768]{2,1,0:T(8,128)(2,1)}, bf1...) custom-call(s32[6,256]{1,0:T(8,128)} %bitcast.3, s32[6,256]{1,0:T(8,128)} %bitcast.4, bf16[256,2560]{1,0:T(8,128)(2,1)} %sh_h.1, ...), custom_call_target="tpu_custom_call" | custom-call | tf_op jit(solution)/shard_map/backward_tail/pallas_call | solution.py:509
  85.3 5.4 %finish.1 = (bf16[256,2560]{1,0:T(8,128)(2,1)}, bf16[6,256]{1,0:T(8,128)(2,1)}, f32[1,160,768]{2,1,0:T(8,128)}, bf16[1,160,768]{2,1,0:T(8,128)(2,1)}, bf16[1,160...) custom-call(bf16[256,2560]{1,0:T(8,128)(2,1)} %get-tuple-element.18.refs_0_, bf16[6,256]{1,0:T(8,128)(2,1)} %get-tuple-element.19.refs_1_, ...), custom_call_target="tpu_custom_call" | custom-call | tf_op jit(solution)/shard_map/finish/pallas_call | solution.py:519

commit v3 on v2

--- a/solution.py
+++ b/solution.py
@@ -29,7 +29,7 @@
 BF16 = jnp.bfloat16
 
 
-PIECES = ((0, 80), (80, 80))
+PIECES = ((0, 48), (48, 32), (80, 48), (128, 32))
 NQ = len(PIECES)
 
 
@@ -171,7 +171,7 @@
     def sc_copy(i):
         to = lax.rem(ep + i, EP)
         return pltpu.make_async_remote_copy(
-            src_ref=sc_tile, dst_ref=sc_recv.at[ep], send_sem=sc_s.at[i], recv_sem=sc_r.at[i],
+            src_ref=sc_tile, dst_ref=sc_recv.at[ep], send_sem=sc_s, recv_sem=sc_r,
             device_id=(to, dp), device_id_type=MESH)
 
     sc_recv[ep] = sc_tile[...]
@@ -190,8 +190,16 @@
         to = lax.rem(ep + n, EP)
         src, dst = groups[i][:2]
         return pltpu.make_async_remote_copy(
-            src_ref=src.at[to], dst_ref=dst.at[ep], send_sem=a2_s.at[i, n], recv_sem=a2_r.at[i, n],
+            src_ref=src.at[to], dst_ref=dst.at[ep], send_sem=a2_s.at[i], recv_sem=a2_r.at[i],
             device_id=(to, dp), device_id_type=MESH)
+
+    def a2_all(i, sem):
+        ref = groups[i][1].at[pl.ds(0, EP - 1)]
+        return pltpu.make_async_copy(ref, ref, sem.at[i])
+
+    def sc_all(sem):
+        ref = sc_recv.at[pl.ds(0, EP - 1)]
+        return pltpu.make_async_copy(ref, ref, sem)
 
     def rows_send(i, first, last, odd_step):
         def send(n, carry):
@@ -250,7 +258,7 @@
     ag_wait(0, 2)
     ag_go(8, 9, 10, 13)
     ag_wait(4)
-    ag_go(14, 15, 18)
+    ag_go(14, 18)
 
     lax.fori_loop(0, 2, r1_wait, 0)
     for q in range(NQ):
@@ -285,7 +293,7 @@
     ag_wait(1, 3)
     ag_go(11, 12)
     ag_wait(5)
-    ag_go(16, 17, 19)
+    ag_go(17, 16, 15, 19)
     ag_wait(10, 11, 12, 13)
     rows_out(1, later=True)
 
@@ -322,20 +330,21 @@
         (x2, 1, yp), (x2, 1, sib), (yp, 1, sib), (yxr, 1, sib), (yxl, 1, sib), (yx2, 1, sib),
     )
 
-    def ng(op):
-        slot, q, to = ng_plan[op]
+    def ng(op, pair_of):
+        slot, kind, to = ng_plan[op]
+        q = 2 * pair_of + kind
         ref = nw_o.at[0, rows_of(slot, q)]
         src = nw_v.at[piece_of(q)] if slot is dp else ref
-        return remote(src, ref, ng_s.at[op], ng_r.at[op], to)
-
-    def ng_go(*ops):
+        return remote(src, ref, ng_s.at[op, pair_of], ng_r.at[op, pair_of], to)
+
+    def ng_go(pair_of, *ops):
         for op in ops:
-            ng(op).start()
-
-    def ng_hop(*moves):
+            ng(op, pair_of).start()
+
+    def ng_hop(pair_of, *moves):
         for arrived, *onward in moves:
-            ng(arrived).wait_recv()
-            ng_go(*onward)
+            ng(arrived, pair_of).wait_recv()
+            ng_go(pair_of, *onward)
 
     def step(q):
         for n in range(3):
@@ -361,14 +370,26 @@
 
         lax.fori_loop(0, size // 16, adam, 0)
 
+    def a2_sent(i):
+        a2_all(i, a2_s).wait()
+
+    def ag_sent():
+        for op in range(len(plan)):
+            ag(op).wait_send()
+
+    def sums_sent():
+        for c in range(NCH):
+            r1_copy(c).wait_send()
+        for q in range(NQ):
+            r2_copy(q).wait_send()
+            for n in range(3):
+                r3_copy(n, q).wait_send()
+        sc_all(sc_s).wait()
+
     def tokens(i):
         _, got, col, width = groups[i]
 
-        def arrived(n, carry):
-            a2_copy(i, n).wait_recv()
-            return carry
-
-        lax.fori_loop(1, EP, arrived, 0)
+        a2_all(i, a2_r).wait()
         rows = got[...].astype(F32).reshape(ROWS, width).astype(BF16)
         routed = jnp.dot(comb[...], rows, preferred_element_type=F32)
         cols = pl.ds(pl.multiple_of(col, 128), width)
@@ -376,11 +397,7 @@
         store(gi_v.at[:, cols], gi_o.at[:, cols])
 
     def scores_out():
-        def got_score(n, carry):
-            sc_copy(n).wait_recv()
-            return carry
-
-        lax.fori_loop(1, EP, got_score, 0)
+        sc_all(sc_r).wait()
         source = lax.broadcasted_iota(jnp.int32, (EP, EP, 128), 1)
         mine = jnp.sum(jnp.where(source == ep, sc_recv[...].astype(F32), 0.0), axis=1).astype(BF16)
         row_e = lax.broadcasted_iota(jnp.int32, (EP, TOK), 0)
@@ -405,11 +422,12 @@
     ag_go(26, 27)
     ag_wait(26, 27)
     rows_out(2)
-    ag_wait(14, 15)
-    ag_go(20, 22, 24)
+    ag_wait(14, 17)
+    ag_go(20, 21, 22, 25)
     over_x(0)
-    ag_wait(16, 17)
-    ag_go(21, 23, 25)
+    over_x(1)
+    ag_wait(15, 16)
+    ag_go(24, 23)
     ag_wait(18, 19, 22, 23, 24, 25)
     rows_out(3)
     rows_send(0, 0, EP // 2, 1)
@@ -417,44 +435,46 @@
     scores_out()
     ag_wait(20, 21)
     ag_go(28, 29)
-    over_x(1)
+    over_x(2)
+    over_x(3)
     ag_wait(28, 29)
     rows_out(4)
     step(0)
-    ng_go(0, 1, 2, 3)
+    ng_go(0, 0, 1, 2, 3)
     step(1)
-    ng_go(15, 16, 17, 18)
-    ng_hop((0, 4, 5), (2, 7, 8, 9), (16, 19, 20, 21), (15, 22, 23), (1, 6))
+    ng_go(0, 15, 16, 17, 18)
+    step(2)
+    ng_go(1, 0, 1, 2, 3)
+    ng_hop(0, (0, 4, 5), (2, 7, 8, 9), (16, 19, 20, 21), (15, 22, 23), (1, 6))
+    step(3)
+    ng_go(1, 15, 16, 17, 18)
+    ng_hop(1, (0, 4, 5), (2, 7, 8, 9), (16, 19, 20, 21), (15, 22, 23), (1, 6))
     tokens(0)
+    ag_sent()
+    ng_hop(0, (8, 10, 12), (19, 24, 25), (7, 11), (4, 13), (17, 26), (20, 27), (22, 28))
     tokens(1)
-    ng_hop((8, 10, 12), (19, 24, 25), (7, 11), (4, 13), (17, 26), (20, 27), (22, 28))
+    a2_sent(0)
+    a2_sent(1)
+    a2_sent(2)
+    ng_hop(1, (8, 10, 12), (19, 24, 25), (7, 11), (4, 13), (17, 26), (20, 27), (22, 28))
     store(nw_v, nw_o.at[0, rows_of(dp)])
     store(nm_v, nm_o.at[0])
     store(nf_v, nf_o.at[0])
     store(ns_v, ns_o.at[0])
     tokens(2)
-    ng_hop((10, 14), (24, 29))
+    ng_hop(0, (10, 14), (24, 29))
+    ng_hop(1, (10, 14), (24, 29))
     tokens(3)
+    sums_sent()
+    a2_sent(3)
     tokens(4)
-    ng_hop(*((op,) for op in (3, 5, 6, 9, 11, 12, 13, 14, 18, 21, 23, 25, 26, 27, 28, 29)))
-
-    for op in range(len(plan)):
-        ag(op).wait_send()
-        ng(op).wait_send()
-
-    def sent(n, carry):
-        for i in range(len(groups)):
-            a2_copy(i, n).wait_send()
-        sc_copy(n).wait_send()
-        return carry
-
-    lax.fori_loop(1, EP, sent, 0)
-    for c in range(NCH):
-        r1_copy(c).wait_send()
-    for q in range(NQ):
-        r2_copy(q).wait_send()
-        for n in range(3):
-            r3_copy(n, q).wait_send()
+    for n in range(2):
+        ng_hop(n, *((op,) for op in (3, 5, 6, 9, 11, 12, 13, 14, 18, 21, 23, 25, 26, 27, 28, 29)))
+
+    a2_sent(4)
+    for op in range(len(ng_plan)):
+        for n in range(2):
+            ng(op, n).wait_send()
     for c in outs:
         c.wait()
 
@@ -497,9 +517,9 @@
         V((3, EP, CAP, CHUNK), BF16), V((3, EP, CAP, CHUNK), BF16),
         V((TOK, D), BF16), V((TOP, TOK), BF16), V((BLK, H), F32), V((BLK, H), BF16),
         V((BLK, H), BF16), V((BLK, H), BF16),
-        dma((13,)), dma((10,)), dma((30,)), dma((30,)), dma((5, EP)), dma((5, EP)),
-        dma((EP,)), dma((EP,)), dma((NCH,)), dma((NCH,)), dma((NQ,)), dma((NQ,)), dma((3, NQ)), dma((3, NQ)),
-        dma((30,)), dma((30,)),
+        dma((13,)), dma((10,)), dma((30,)), dma((30,)), dma((5,)), dma((5,)),
+        dma, dma, dma((NCH,)), dma((NCH,)), dma((NQ,)), dma((NQ,)), dma((3, NQ)), dma((3, NQ)),
+        dma((30, 2)), dma((30, 2)),
     ]
     shapes = [
         jax.ShapeDtypeStruct((TOK, D), BF16), jax.ShapeDtypeStruct((TOP, TOK), BF16),

time: 90.8 us -> 87.7 us (0.966)
  Pallas kernels: 90.1 us -> 86.9 us
    pallas_call x1, Pallas kernels: 84.7 us -> 81.5 us  [per_device(): pl.pallas_call(kernel, out_shape=shapes, in_specs=[any_spec] * 13, out_sp...]
where the time goes in v3:
time: 87.7 us; the launch traced here: 87.6 us
  Pallas kernels  86.9 us (99%)
    pallas_call x1, Pallas kernels, per_device(): pl.pallas_call(kernel, out_shape=shapes, in_specs=[any_spec] * 13, out_sp...  81.5 us
    pallas_call x1, Pallas kernels, per_device(): pl.pallas_call(finish, out_shape=shapes, in_specs=[any_spec] * 6, out_spe...  5.36 us

profile of v3, /device:TPU:1, one launch (start us, length us, event | category | flops | bytes accessed | tf_op | source)
XLA Modules:
  0.0 87.6 jit_solution(3939602317944690062)
XLA Ops:
  0.6 81.5 %backward_tail.1 = (bf16[256,2560]{1,0:T(8,128)(2,1)}, bf16[6,256]{1,0:T(8,128)(2,1)}, f32[1,160,768]{2,1,0:T(8,128)}, bf16[1,160,768]{2,1,0:T(8,128)(2,1)}, bf1...) custom-call(s32[6,256]{1,0:T(8,128)} %bitcast.3, s32[6,256]{1,0:T(8,128)} %bitcast.4, bf16[256,2560]{1,0:T(8,128)(2,1)} %sh_h.1, ...), custom_call_target="tpu_custom_call" | custom-call | tf_op jit(solution)/shard_map/backward_tail/pallas_call | solution.py:529
  82.2 5.4 %finish.1 = (bf16[256,2560]{1,0:T(8,128)(2,1)}, bf16[6,256]{1,0:T(8,128)(2,1)}, f32[1,160,768]{2,1,0:T(8,128)}, bf16[1,160,768]{2,1,0:T(8,128)(2,1)}, bf16[1,160...) custom-call(bf16[256,2560]{1,0:T(8,128)(2,1)} %get-tuple-element.18.refs_0_, bf16[6,256]{1,0:T(8,128)(2,1)} %get-tuple-element.19.refs_1_, ...), custom_call_target="tpu_custom_call" | custom-call | tf_op jit(solution)/shard_map/finish/pallas_call | solution.py:539

commit v4 on v3

--- a/solution.py
+++ b/solution.py
@@ -251,9 +251,9 @@
         rows = piece_of(q)
         return remote(r2_send.at[:, rows], r2_recv.at[:, rows], r2_s.at[q], r2_r.at[q], yp)
 
-    lax.fori_loop(0, 2, weight_part, 0)
     ag_wait(6, 7)
     rows_out(0, later=True)
+    lax.fori_loop(0, 2, weight_part, 0)
     lax.fori_loop(2, NCH, weight_part, 0)
     ag_wait(0, 2)
     ag_go(8, 9, 10, 13)

time: 87.7 us -> 87.7 us (level)
  no operation moved by 1% of the time
where the time goes in v4:
time: 87.7 us; the launch traced here: 87.6 us
  Pallas kernels  86.9 us (99%)
    pallas_call x1, Pallas kernels, per_device(): pl.pallas_call(kernel, out_shape=shapes, in_specs=[any_spec] * 13, out_sp...  81.5 us
    pallas_call x1, Pallas kernels, per_device(): pl.pallas_call(finish, out_shape=shapes, in_specs=[any_spec] * 6, out_spe...  5.36 us

profile of v4, /device:TPU:1, one launch (start us, length us, event | category | flops | bytes accessed | tf_op | source)
XLA Modules:
  0.0 87.6 jit_solution(12504463946659309956)
XLA Ops:
  0.6 81.5 %backward_tail.1 = (bf16[256,2560]{1,0:T(8,128)(2,1)}, bf16[6,256]{1,0:T(8,128)(2,1)}, f32[1,160,768]{2,1,0:T(8,128)}, bf16[1,160,768]{2,1,0:T(8,128)(2,1)}, bf1...) custom-call(s32[6,256]{1,0:T(8,128)} %bitcast.3, s32[6,256]{1,0:T(8,128)} %bitcast.4, bf16[256,2560]{1,0:T(8,128)(2,1)} %sh_h.1, ...), custom_call_target="tpu_custom_call" | custom-call | tf_op jit(solution)/shard_map/backward_tail/pallas_call | solution.py:529
  82.2 5.4 %finish.1 = (bf16[256,2560]{1,0:T(8,128)(2,1)}, bf16[6,256]{1,0:T(8,128)(2,1)}, f32[1,160,768]{2,1,0:T(8,128)}, bf16[1,160,768]{2,1,0:T(8,128)(2,1)}, bf16[1,160...) custom-call(bf16[256,2560]{1,0:T(8,128)(2,1)} %get-tuple-element.18.refs_0_, bf16[6,256]{1,0:T(8,128)(2,1)} %get-tuple-element.19.refs_1_, ...), custom_call_target="tpu_custom_call" | custom-call | tf_op jit(solution)/shard_map/finish/pallas_call | solution.py:539
